TPU v7x, 32 devices: a whole 2x2x4 slice. The times are simulated.
32 devices in a mesh: thick: 4 (over y, core), wide: 8 (over z, x).
Axes of the slice: x: 2, y: 2, z: 4, core: 2. Of those that a mesh axis runs over, the one named last changes fastest.
Arguments:
- phase_in: float32 [128, 512, 512], P('thick', 'wide'), may hold values from -1 to 1
- density_in: float32 [128, 512, 512], P('thick', 'wide'), may hold values from 0 to 1
Outputs:
- phase_out: float32 [128, 512, 512], P('thick', 'wide')
- density_out: float32 [128, 512, 512], P('thick', 'wide')
- mean_flux: float32 [], replicated
All inputs are finite; a program needn't handle non-finite values.
Results may differ from a plain program's by a relative error of at most 0.0001.
Values sent between devices are 32-bit elements; how exact they have to be, the bound alone decides.
A program may use at most 192 MiB of HBM per device.

v0:
```python
import math
import jax
import jax.numpy as jnp
from jax import lax
from jax.sharding import PartitionSpec as P

NX = 512
NY = 512
NZ = 128
DIFF_STEPS = 3
time_step = 100.0
stabilizer = 3.0
gradient_energy = 2.0
walk_step = 0.16


def with_halo(array, sides, width):
    for axis, dim in sides:
        peers, length = (lax.axis_size(axis), array.shape[dim])
        up = [(i, (i + 1) % peers) for i in range(peers)]
        down = [(j, i) for i, j in up]
        last = lax.slice_in_dim(array, length - width, length, axis=dim)
        leading = lax.slice_in_dim(array, 0, width, axis=dim)
        before = lax.ppermute(last, axis, up)
        after = lax.ppermute(leading, axis, down)
        array = jnp.concatenate([before, array, after], axis=dim)
    return array


def tables(length):
    index = jnp.arange(length, dtype=jnp.int32)
    folded = index[:, None] * index[None, :] % length
    angle = folded.astype(jnp.float32) * (2.0 * math.pi / length)
    return (jnp.cos(angle), jnp.sin(angle))


def squared_wave(index, length):
    signed = jnp.where(index < length // 2, index, index - length).astype(jnp.float32)
    return (signed * (2.0 * math.pi / length)) ** 2


def product(form, left, right):
    return jnp.einsum(form, left, right, precision=lax.Precision.HIGHEST)


def advance(density, conduct):
    centre = density[1:-1, 1:-1]
    middle = conduct[1:-1, 1:-1]

    def inflow(near_density, near_conduct):
        return 0.5 * (near_conduct + middle) * (near_density - centre)

    lower = inflow(density[:-2, 1:-1], conduct[:-2, 1:-1])
    total = lower + inflow(density[2:, 1:-1], conduct[2:, 1:-1])
    total = (
        total
        + inflow(density[1:-1, :-2], conduct[1:-1, :-2])
        + inflow(density[1:-1, 2:], conduct[1:-1, 2:])
    )
    total = (
        total
        + inflow(jnp.roll(centre, 1, 2), jnp.roll(middle, 1, 2))
        + inflow(jnp.roll(centre, -1, 2), jnp.roll(middle, -1, 2))
    )
    return (centre + walk_step * total, lower)


def per_device(phase_in, density_in):
    wide_count = lax.axis_size("wide")
    thick_count = lax.axis_size("thick")
    y_share = NY // wide_count
    x_share = NX // thick_count
    cosine_y, sine_y = tables(NY)
    cosine_x, sine_x = tables(NX)
    cosine_z, sine_z = tables(NZ)
    wave_y = squared_wave(
        lax.axis_index("wide") * y_share + jnp.arange(y_share, dtype=jnp.int32), NY
    )
    wave_x = squared_wave(
        lax.axis_index("thick") * x_share + jnp.arange(x_share, dtype=jnp.int32), NX
    )
    wave_z = squared_wave(jnp.arange(NZ, dtype=jnp.int32), NZ)
    wave = wave_y[:, None, None] + wave_z[None, :, None] + wave_x[None, None, :]
    implicit = 1.0 + time_step * stabilizer * wave + time_step * gradient_energy * wave * wave
    factor = 1.0 / (NX * NY * NZ)
    keep = (1.0 + time_step * stabilizer * wave) / implicit * factor
    drive = -time_step * wave / implicit * factor
    phase = phase_in
    chemical = phase * phase * phase - phase
    form = "fzxy,yk->fzxk"
    fields = jnp.stack([phase, chemical])
    real_part = product(form, fields, cosine_y)
    imag_part = -product(form, fields, sine_y)
    pair = (
        lax.all_to_all(real_part, "wide", split_axis=3, concat_axis=2, tiled=True),
        lax.all_to_all(imag_part, "wide", split_axis=3, concat_axis=2, tiled=True),
    )
    forward_real_part, forward_imag_part = pair
    form = "fzxy,xk->fzyk"
    out_real = product(form, forward_real_part, cosine_x) + product(form, forward_imag_part, sine_x)
    out_imag = product(form, forward_imag_part, cosine_x) - product(form, forward_real_part, sine_x)
    pair = (
        lax.all_to_all(out_real, "thick", split_axis=3, concat_axis=1, tiled=True),
        lax.all_to_all(out_imag, "thick", split_axis=3, concat_axis=1, tiled=True),
    )
    real_part, imag_part = pair
    form = "fzyk,zw->fywk"
    forward_out_real = product(form, real_part, cosine_z) + product(form, imag_part, sine_z)
    forward_out_imag = product(form, imag_part, cosine_z) - product(form, real_part, sine_z)
    real_part = forward_out_real
    imag_part = forward_out_imag
    new_real = keep * real_part[0] + drive * real_part[1]
    new_imag = keep * imag_part[0] + drive * imag_part[1]
    form = "ywk,wz->yzk"
    depth_real = product(form, new_real, cosine_z) - product(form, new_imag, sine_z)
    depth_imag = product(form, new_imag, cosine_z) + product(form, new_real, sine_z)
    real_part = lax.all_to_all(depth_real, "thick", split_axis=1, concat_axis=2, tiled=True)
    imag_part = lax.all_to_all(depth_imag, "thick", split_axis=1, concat_axis=2, tiled=True)
    form = "yzk,kx->zxy"
    out_real = product(form, real_part, cosine_x) - product(form, imag_part, sine_x)
    out_imag = product(form, imag_part, cosine_x) + product(form, real_part, sine_x)
    pair = (out_real, out_imag)
    real_part = lax.all_to_all(pair[0], "wide", split_axis=1, concat_axis=2, tiled=True)
    imag_part = lax.all_to_all(pair[1], "wide", split_axis=1, concat_axis=2, tiled=True)
    form = "zxk,ky->zxy"
    phase = product(form, real_part, cosine_y) - product(form, imag_part, sine_y)
    conduct = 0.05 + 0.95 * jax.nn.sigmoid(4.0 * phase)
    position = lax.axis_index("thick")
    final = thick_count - 1

    def pin_density(density, margin):
        depth = density.shape[0]
        layer = jnp.arange(depth, dtype=jnp.int32)[:, None, None]
        density = jnp.where((position == 0) & (layer < margin), 1.0, density)
        return jnp.where((position == final) & (layer >= depth - margin), 0.0, density)

    density = density_in
    lower = jnp.zeros_like(density)
    conduct_ext = with_halo(conduct, (("thick", 0), ("wide", 1)), 1)
    depth = conduct_ext.shape[0]
    layer = jnp.arange(depth, dtype=jnp.int32)[:, None, None]
    first = conduct_ext[1 : 1 + 1]
    last = conduct_ext[depth - 1 - 1 : depth - 1]
    conduct_ext = jnp.where((position == 0) & (layer < 1), first, conduct_ext)
    conduct_ext = jnp.where((position == final) & (layer >= depth - 1), last, conduct_ext)
    for turn in range(DIFF_STEPS):
        padded = pin_density(with_halo(density, (("thick", 0), ("wide", 1)), 1), 1)
        density, lower = advance(padded, conduct_ext)
    flux = lax.psum(jnp.sum(lower), ("thick", "wide")) / (NX * NY)
    return (phase, density, flux)


def solution(mesh):
    in_specs = (P("thick", "wide", None), P("thick", "wide", None))
    out_specs = (P("thick", "wide", None), P("thick", "wide", None), P())
    return jax.shard_map(
        per_device, mesh=mesh, in_specs=in_specs, out_specs=out_specs, check_vma=False
    )
```

profile of v0, /device:TPU:12, one launch (start us, length us, event | category | flops | bytes accessed | tf_op | source)
XLA Modules:
  0.0 1466.6 jit_solution(4611788430884908214)
XLA Ops:
  5.6 32.7 %fusion.1 = f32[2,32,64,512]{3,2,1,0:T(8,128)} fusion(f32[1,32,64,512]{3,2,1,0:T(8,128)S(1)} %fusion.5, f32[1,32,64,512]{3,2,1,0:T(8,128)S(1)} %bitcast.208), kind=kOutput, calls=%fused_computation.12 | convolution fusion | flops 12890669056 | bytes 16777216 | tf_op jit(solution)/shard_map/fzxy,yk->fzxk/dot_general | solution.py:43
  38.3 16.3 %copy.13 = f32[2,32,64,512]{2,1,0,3:T(8,128)} copy(f32[2,32,64,512]{3,2,1,0:T(8,128)} %fusion.1) | data formatting | bytes 16777216 | tf_op jit(solution)/shard_map/fzxy,yk->fzxk/dot_general | solution.py:43
  54.6 15.4 %reshape.91 = f32[8,1,262144]{2,1,0:T(1,128)} reshape(f32[512,2,32,64]{3,2,1,0:T(8,128)} %bitcast.189) | data formatting | bytes 16777216
  76.5 25.5 %fusion.63 = f32[2,32,64,512]{3,2,1,0:T(8,128)} fusion(f32[1,32,64,512]{3,2,1,0:T(8,128)} %copy-done.5, f32[1,32,64,512]{3,2,1,0:T(8,128)} %bitcast.207), kind=kOutput, calls=%fused_computation.115 | convolution fusion | flops 12892766208 | bytes 16777216 | tf_op jit(solution)/shard_map/fzxy,yk->fzxk/dot_general | solution.py:43
  102.0 16.8 %copy.15 = f32[2,32,64,512]{2,1,0,3:T(8,128)} copy(f32[2,32,64,512]{3,2,1,0:T(8,128)} %fusion.63) | data formatting | bytes 16777216 | tf_op jit(solution)/shard_map/neg | solution.py:93
  118.8 15.5 %reshape.93 = f32[8,1,262144]{2,1,0:T(1,128)} reshape(f32[512,2,32,64]{3,2,1,0:T(8,128)} %bitcast.190) | data formatting | bytes 16777216
  134.3 122.8 %all-to-all-done = f32[8,1,262144]{2,1,0:T(1,128)} async-done(((f32[8,1,262144]{2,1,0:T(1,128)}), f32[8,1,262144]{2,1,0:T(1,128)}, u32[]{:S(2)}, u32[]{:S(2)}) %all-to-all-start) | async-done | bytes 8388640 | tf_op jit(solution)/shard_map/all_to_all | solution.py:95
  265.0 26.3 %reduce = f32[8,262144]{1,0:T(8,128)} reduce(f32[8,1,262144]{2,1,0:T(1,128)} %all-to-all-done, f32[]{:T(128)} %broadcast.342), dimensions={1}, to_apply=%all_to_all.104.reduce_sub_computation | reduce | bytes 16777220 | tf_op jit(solution)/shard_map/all_to_all | solution.py:95
  291.2 15.6 %reshape.92 = f32[512,2,32,64]{3,2,1,0:T(8,128)} reshape(f32[8,262144]{1,0:T(8,128)} %reduce) | data formatting | bytes 16777216
  306.9 17.8 %copy.40 = f32[2,32,64,8,64]{2,3,4,1,0:T(8,128)} copy(f32[2,32,64,8,64]{2,1,0,4,3:T(8,128)} %bitcast.195) | data formatting | bytes 16777216 | tf_op jit(solution)/shard_map/all_to_all | solution.py:95
  324.7 14.2 all_to_all.107
  338.9 25.5 %fusion.75 = f32[2,32,64,512]{3,2,1,0:T(8,128)} fusion(f32[2,32,512,64]{2,3,1,0:T(8,128)} %all_to_all.107), kind=kOutput, calls=%fused_computation.133 | convolution fusion | flops 12888571904 | bytes 16777216 | tf_op jit(solution)/shard_map/fzxy,xk->fzyk/dot_general | solution.py:43
  364.5 79.8 %all-to-all-done.1 = f32[8,1,262144]{2,1,0:T(1,128)} async-done(((f32[8,1,262144]{2,1,0:T(1,128)}), f32[8,1,262144]{2,1,0:T(1,128)}, u32[]{:S(2)}, u32[]{:S(2)}) %all-to-all-start.1) | async-done | bytes 8388640 | tf_op jit(solution)/shard_map/all_to_all | solution.py:96
  444.3 26.5 %reduce.1 = f32[8,262144]{1,0:T(8,128)} reduce(f32[8,1,262144]{2,1,0:T(1,128)} %all-to-all-done.1, f32[]{:T(128)} %broadcast.342), dimensions={1}, to_apply=%all_to_all.108.reduce_sub_computation | reduce | bytes 16777220 | tf_op jit(solution)/shard_map/all_to_all | solution.py:96
  470.8 15.6 %reshape.94 = f32[512,2,32,64]{3,2,1,0:T(8,128)} reshape(f32[8,262144]{1,0:T(8,128)} %reduce.1) | data formatting | bytes 16777216
  486.4 17.8 %copy.39 = f32[2,32,64,8,64]{2,3,4,1,0:T(8,128)} copy(f32[2,32,64,8,64]{2,1,0,4,3:T(8,128)} %bitcast.197) | data formatting | bytes 16777216 | tf_op jit(solution)/shard_map/all_to_all | solution.py:96
  504.2 14.7 %all_to_all.111 = f32[2,32,512,64]{2,3,1,0:T(8,128)} reshape(f32[2,32,8,64,64]{3,2,4,1,0:T(8,128)} %bitcast.198) | data formatting | bytes 16777216 | tf_op jit(solution)/shard_map/all_to_all | solution.py:96
  518.9 26.8 %convolution_add_fusion = f32[2,32,64,512]{3,2,1,0:T(8,128)} fusion(f32[2,32,64,512]{3,2,1,0:T(8,128)} %fusion.75, f32[2,32,512,64]{2,3,1,0:T(8,128)} %all_to_all.111), kind=kOutput, calls=%fused_computation.117 | convolution fusion | flops 12890669056 | bytes 25165824 | tf_op jit(solution)/shard_map/fzxy,xk->fzyk/dot_general | solution.py:43
  545.6 16.4 %copy.17 = f32[2,32,64,512]{2,1,0,3:T(8,128)} copy(f32[2,32,64,512]{3,2,1,0:T(8,128)} %convolution_add_fusion) | data formatting | bytes 16777216 | tf_op jit(solution)/shard_map/add | solution.py:100
  562.1 14.3 reshape.95
  582.5 24.2 %fusion.73 = f32[2,32,64,512]{3,2,1,0:T(8,128)S(1)} fusion(f32[2,32,512,64]{2,3,1,0:T(8,128)} %all_to_all.111), kind=kOutput, calls=%fused_computation.131 | convolution fusion | flops 12888571904 | bytes 16777216 | tf_op jit(solution)/shard_map/fzxy,xk->fzyk/dot_general | solution.py:43
  606.8 25.9 %convolution_subtract_fusion = f32[2,32,64,512]{3,2,1,0:T(8,128)} fusion(f32[2,32,64,512]{3,2,1,0:T(8,128)S(1)} %fusion.73, f32[2,32,512,64]{2,3,1,0:T(8,128)} %all_to_all.107), kind=kOutput, calls=%fused_computation.116 | convolution fusion | flops 12890669056 | bytes 25165824 | tf_op jit(solution)/shard_map/fzxy,xk->fzyk/dot_general | solution.py:43
  632.6 16.3 %copy.19 = f32[2,32,64,512]{2,1,0,3:T(8,128)} copy(f32[2,32,64,512]{3,2,1,0:T(8,128)} %convolution_subtract_fusion) | data formatting | bytes 16777216 | tf_op jit(solution)/shard_map/sub | solution.py:101
  648.9 14.4 reshape.97
  663.3 10.8 all-to-all-done.2
  681.7 28.3 %reduce.2 = f32[4,524288]{1,0:T(4,128)} reduce(f32[4,1,524288]{2,1,0:T(1,128)} %all-to-all-done.2, f32[]{:T(128)} %broadcast.342), dimensions={1}, to_apply=%all_to_all.112.reduce_sub_computation | reduce | bytes 16777220 | tf_op jit(solution)/shard_map/all_to_all | solution.py:103
  709.9 16.8 %reshape.96 = f32[512,2,32,64]{3,2,1,0:T(8,128)} reshape(f32[4,524288]{1,0:T(4,128)} %reduce.2) | data formatting | bytes 16777216
  726.7 15.9 %copy.18 = f32[2,32,64,4,128]{4,1,3,2,0:T(8,128)} copy(f32[2,32,64,4,128]{2,1,0,4,3:T(8,128)} %bitcast.193) | data formatting | bytes 16777216 | tf_op jit(solution)/shard_map/all_to_all | solution.py:103
  742.7 12.2 fusion.108
  754.8 18.2 %all-to-all-done.3 = f32[4,1,524288]{2,1,0:T(1,128)} async-done(((f32[4,1,524288]{2,1,0:T(1,128)}), f32[4,1,524288]{2,1,0:T(1,128)}, u32[]{:S(2)}, u32[]{:S(2)}) %all-to-all-start.3) | async-done | bytes 8388640 | tf_op jit(solution)/shard_map/all_to_all | solution.py:104
  773.1 28.6 %reduce.3 = f32[4,524288]{1,0:T(4,128)} reduce(f32[4,1,524288]{2,1,0:T(1,128)} %all-to-all-done.3, f32[]{:T(128)} %broadcast.342), dimensions={1}, to_apply=%all_to_all.116.reduce_sub_computation | reduce | bytes 16777220 | tf_op jit(solution)/shard_map/all_to_all | solution.py:104
  801.7 16.8 %reshape.98 = f32[512,2,32,64]{3,2,1,0:T(8,128)} reshape(f32[4,524288]{1,0:T(4,128)} %reduce.3) | data formatting | bytes 16777216
  818.5 15.8 %copy.20 = f32[2,32,64,4,128]{4,1,3,2,0:T(8,128)} copy(f32[2,32,64,4,128]{2,1,0,4,3:T(8,128)} %bitcast.194) | data formatting | bytes 16777216 | tf_op jit(solution)/shard_map/all_to_all | solution.py:104
  834.3 11.3 fusion.106
  845.6 12.3 add_bitcast_fusion
  858.0 10.2 subtract_bitcast_fusion
  891.6 8.6 fusion.112
  900.2 8.6 add_bitcast_fusion.2
  913.3 24.9 %all-to-all-done.4 = f32[64,128,128]{2,0,1:T(8,128)} async-done(((f32[64,128,128]{2,0,1:T(8,128)}), f32[64,128,128]{2,0,1:T(8,128)}, u32[]{:S(2)}, u32[]{:S(2)}) %all-to-all-start.4) | async-done | bytes 4194336 | tf_op jit(solution)/shard_map/all_to_all | solution.py:117
  944.9 7.8 copy.44
  958.1 14.3 fusion.82
  972.5 19.0 %all-to-all-done.5 = f32[64,128,128]{2,0,1:T(8,128)} async-done(((f32[64,128,128]{2,0,1:T(8,128)}), f32[64,128,128]{2,0,1:T(8,128)}, u32[]{:S(2)}, u32[]{:S(2)}) %all-to-all-start.5) | async-done | bytes 4194336 | tf_op jit(solution)/shard_map/all_to_all | solution.py:118
  991.5 7.8 copy.43
  1004.7 14.9 %subtract_bitcast_fusion.1 = f32[32,512,64]{1,2,0:T(8,128)} fusion(f32[512,64,32]{0,1,2:T(8,128)} %fusion.82, f32[64,32,512]{2,0,1:T(8,128)} %all_to_all.127), kind=kOutput, calls=%fused_computation.112 | convolution fusion | flops 6447169536 | bytes 12582912 | tf_op jit(solution)/shard_map/yzk,kx->zxy/dot_general | solution.py:43
  1019.6 9.2 copy.25
  1028.8 9.8 reshape.99
  1046.0 12.6 fusion.78
  1058.7 12.4 add_bitcast_fusion.1
  1071.0 9.2 copy.27
  1080.2 9.9 reshape.101
  1090.1 46.9 %all-to-all-done.6 = f32[8,1,131072]{2,1,0:T(1,128)} async-done(((f32[8,1,131072]{2,1,0:T(1,128)}), f32[8,1,131072]{2,1,0:T(1,128)}, u32[]{:S(2)}, u32[]{:S(2)}) %all-to-all-start.6) | async-done | bytes 4194336 | tf_op jit(solution)/shard_map/all_to_all | solution.py:123
  1150.1 14.0 reduce.4
  1164.1 8.7 reshape.100
  1172.8 11.6 copy.42
  1191.8 14.5 fusion.80
  1206.3 28.0 %all-to-all-done.7 = f32[8,1,131072]{2,1,0:T(1,128)} async-done(((f32[8,1,131072]{2,1,0:T(1,128)}), f32[8,1,131072]{2,1,0:T(1,128)}, u32[]{:S(2)}, u32[]{:S(2)}) %all-to-all-start.7) | async-done | bytes 4194336 | tf_op jit(solution)/shard_map/all_to_all | solution.py:124
  1234.3 14.2 reduce.5
  1248.5 8.8 reshape.102
  1257.3 11.5 copy.41
  1276.3 24.5 %multiply_add_fusion = (f32[32,64,512]{2,1,0:T(8,128)S(1)}, f32[32,64,512]{2,1,0:T(8,128)}) fusion(f32[32,64,512]{2,1,0:T(8,128)} %fusion.80, f32[32,64,512]{2,1,0:T(8,128)} %all_to_all.135), kind=kOutput, calls=%fused_computation.110 | convolution fusion | flops 6453460992 | bytes 16777216 | tf_op jit(solution)/shard_map/zxk,ky->zxy/dot_general | solution.py:43
  1334.5 16.4 %fusion.39 = (f32[32,64,512]{2,1,0:T(8,128)}, f32[32,64,512]{2,1,0:T(8,128)}, f32[32,64,512]{2,1,0:T(8,128)}, f32[32,64,512]{2,1,0:T(8,128)}) fusion(f32[34,66,512]{2,1,0:T(8,128)S(1)} %get-tuple-element.44, f32[32,64,511]{2,1,0:T(8,128)} %get-tuple-element.49, f32[32,64,1]{2,1,0:T(8,128)} %get-tuple-element.47, f32[32,64,1]{2,1,0:T(8,128)} %get-tuple-element.48, ...), kind=kLoop, calls=%fused_computation.65 | loop fusion | flops 36700160 | bytes 75497472 | tf_op jit(solution)/shard_map/add | solution.py:65
  1377.6 10.6 fusion.28
  1409.9 11.6 fusion.224
  1421.5 42.8 %psum.7 = f32[]{:T(128)} all-reduce(f32[]{:T(128)} %get-tuple-element.7), channel_id=1, replica_groups=mesh['thick'=4,'wide'=8] {'thick','wide'}, use_global_device_ids=true, to_apply=%region_1.2 | all-reduce | flops 1 | bytes 8 | tf_op jit(solution)/shard_map/psum | solution.py:149
  (108 shorter events, 195.9 us)
Async XLA Ops:
  0.6 4.9 copy-start.4
  3.5 2.0 copy-start.5
  70.0 187.1 %all-to-all-start = ((f32[8,1,262144]{2,1,0:T(1,128)}), f32[8,1,262144]{2,1,0:T(1,128)}, u32[]{:S(2)}, u32[]{:S(2)}) async-start(f32[8,1,262144]{2,1,0:T(1,128)} %reshape.91), calls=%async_computation | async-start | bytes 16777216 | tf_op jit(solution)/shard_map/all_to_all | solution.py:95
  257.1 187.2 %all-to-all-start.1 = ((f32[8,1,262144]{2,1,0:T(1,128)}), f32[8,1,262144]{2,1,0:T(1,128)}, u32[]{:S(2)}, u32[]{:S(2)}) async-start(f32[8,1,262144]{2,1,0:T(1,128)} %reshape.93), calls=%async_computation.1 | async-start | bytes 16777216 | tf_op jit(solution)/shard_map/all_to_all | solution.py:96
  576.4 97.7 %all-to-all-start.2 = ((f32[4,1,524288]{2,1,0:T(1,128)}), f32[4,1,524288]{2,1,0:T(1,128)}, u32[]{:S(2)}, u32[]{:S(2)}) async-start(f32[4,1,524288]{2,1,0:T(1,128)} %reshape.95), calls=%async_computation.2 | async-start | bytes 16777216 | tf_op jit(solution)/shard_map/all_to_all | solution.py:103
  674.1 99.0 %all-to-all-start.3 = ((f32[4,1,524288]{2,1,0:T(1,128)}), f32[4,1,524288]{2,1,0:T(1,128)}, u32[]{:S(2)}, u32[]{:S(2)}) async-start(f32[4,1,524288]{2,1,0:T(1,128)} %reshape.97), calls=%async_computation.3 | async-start | bytes 16777216 | tf_op jit(solution)/shard_map/all_to_all | solution.py:104
  834.3 11.3 copy-start
  834.3 23.7 %slice-start = ((s8[8388608]{0:T(1024)(128)(4,1)}), s8[4194304]{0:T(1024)(128)(4,1)S(1)}, s32[]{:S(2)}) async-start(s8[8388608]{0:T(1024)(128)(4,1)} %bitcast.184), calls=%async_computation.8 | async-start | bytes 8388608
  845.6 12.4 slice-start.1
  858.0 10.2 copy-start.6
  868.2 5.8 copy-start.7
  885.1 53.1 %all-to-all-start.4 = ((f32[64,128,128]{2,0,1:T(8,128)}), f32[64,128,128]{2,0,1:T(8,128)}, u32[]{:S(2)}, u32[]{:S(2)}) async-start(f32[64,128,128]{2,0,1:T(8,128)} %copy.21), calls=%async_computation.4 | async-start | bytes 8388608 | tf_op jit(solution)/shard_map/all_to_all | solution.py:117
  938.2 53.3 %all-to-all-start.5 = ((f32[64,128,128]{2,0,1:T(8,128)}), f32[64,128,128]{2,0,1:T(8,128)}, u32[]{:S(2)}, u32[]{:S(2)}) async-start(f32[64,128,128]{2,0,1:T(8,128)} %copy.23), calls=%async_computation.5 | async-start | bytes 8388608 | tf_op jit(solution)/shard_map/all_to_all | solution.py:118
  1038.6 98.4 %all-to-all-start.6 = ((f32[8,1,131072]{2,1,0:T(1,128)}), f32[8,1,131072]{2,1,0:T(1,128)}, u32[]{:S(2)}, u32[]{:S(2)}) async-start(f32[8,1,131072]{2,1,0:T(1,128)} %reshape.99), calls=%async_computation.6 | async-start | bytes 8388608 | tf_op jit(solution)/shard_map/all_to_all | solution.py:123
  1046.0 12.7 copy-start.1
  1137.0 97.2 %all-to-all-start.7 = ((f32[8,1,131072]{2,1,0:T(1,128)}), f32[8,1,131072]{2,1,0:T(1,128)}, u32[]{:S(2)}, u32[]{:S(2)}) async-start(f32[8,1,131072]{2,1,0:T(1,128)} %reshape.101), calls=%async_computation.7 | async-start | bytes 8388608 | tf_op jit(solution)/shard_map/all_to_all | solution.py:124
  1145.0 4.4 collective-permute-start
  1145.1 157.1 %collective-permute-start.1 = (f32[1,64,512]{2,1,0:T(8,128)S(1)}, f32[1,64,512]{2,1,0:T(8,128)S(1)}, u32[]{:S(2)}, u32[]{:S(2)}) collective-permute-start(f32[1,64,512]{2,1,0:T(8,128)S(1)} %get-tuple-element.41), channel_id=1, source_target_pairs={{8,0},{16,8},{24,16},{0,24},{9,1},{17,9},{25,17},{1,25},{10,2},{18... | collective-permute-start | bytes 393224 | tf_op jit(solution)/shard_map/ppermute | solution.py:25
  1268.7 32.9 %slice-start.2 = ((s8[4456448]{0:T(1024)(128)(4,1)}), s8[262144]{0:T(1024)(128)(4,1)S(1)}, s32[]{:S(2)}) async-start(s8[4456448]{0:T(1024)(128)(4,1)} %bitcast.209), calls=%async_computation.10 | async-start | bytes 524288
  1276.2 25.4 %slice-start.3 = ((s8[4456448]{0:T(1024)(128)(4,1)}), s8[4194304]{0:T(1024)(128)(4,1)S(1)}, s32[]{:S(2)}) async-start(s8[4456448]{0:T(1024)(128)(4,1)} %bitcast.209), calls=%async_computation.11 | async-start | bytes 8388608
  1276.3 25.4 %copy-start.9 = (f32[32,64,512]{2,1,0:T(8,128)S(1)}, f32[32,64,512]{2,1,0:T(8,128)}, u32[]{:S(2)}) copy-start(f32[32,64,512]{2,1,0:T(8,128)} %param.3) | copy-start | bytes 12582916
  1300.7 4.6 collective-permute-start.5
  1301.7 5.1 collective-permute-start.4
  1302.2 14.2 copy-start.8
  1306.9 6.2 collective-permute-start.7
  1310.0 5.3 collective-permute-start.6
  1310.2 6.3 collective-permute-start.3
  1313.1 5.2 collective-permute-start.2
  1350.9 17.4 %copy-start.2 = (f32[32,64,512]{2,1,0:T(8,128)S(1)}, f32[32,64,512]{2,1,0:T(8,128)}, u32[]{:S(2)}) copy-start(f32[32,64,512]{2,1,0:T(8,128)} %get-tuple-element.3) | copy-start | bytes 12582916
  1352.1 3.7 collective-permute-start.9
  1352.1 5.1 collective-permute-start.8
  1358.6 4.7 collective-permute-start.11
  1361.3 7.0 collective-permute-start.10
  1388.2 3.7 collective-permute-start.13
  1388.3 5.1 collective-permute-start.12
  1393.5 4.4 collective-permute-start.15
  1395.5 5.2 collective-permute-start.14
  1404.7 5.2 copy-start.3
where the time goes:
time: 1480 us; the launch traced here: 1470 us
  local copies, waits for them, and re-layouts  443 us (30%)
  waiting for transfers between devices  383 us (26%)
  matrix products  329 us (22%)
  other arithmetic  196 us (13%)
  starting transfers between devices  69.8 us (5%)
  blocking collectives  42.8 us (3%)
    dot_general x20, matrix products, product(): return jnp.einsum(form, left, right, precision=lax.Precision.HIGHEST)  329 us
    unnamed x42, local copies, waits for them, and re-layouts  165 us
    all_to_all x1, waiting for transfers between devices, per_device(): lax.all_to_all(real_part, 'wide', split_axis=3, concat_axis=2, tiled=True)  123 us
    all_to_all x1, waiting for transfers between devices, per_device(): lax.all_to_all(imag_part, 'wide', split_axis=3, concat_axis=2, tiled=True)  79.8 us
    all_to_all x1, waiting for transfers between devices, per_device(): lax.all_to_all(pair[0], 'wide', split_axis=1, concat_axis=2, tiled=True)  46.9 us
    psum x1, blocking collectives, per_device(): flux = lax.psum(jnp.sum(lower), ('thick', 'wide')) / (NX * NY)  42.8 us
    all_to_all x3, local copies, waits for them, and re-layouts, per_device(): lax.all_to_all(real_part, 'wide', split_axis=3, concat_axis=2, tiled=True)  32.6 us
    all_to_all x2, local copies, waits for them, and re-layouts, per_device(): lax.all_to_all(imag_part, 'wide', split_axis=3, concat_axis=2, tiled=True)  32.5 us
  transfers between devices with their start and end apart: 24, of which 21 were waited for; matrix products, arithmetic and copies ran while one was open for 34% of the time, Pallas kernels for 0%

commit v1 on v0

--- a/solution.py
+++ b/solution.py
@@ -12,6 +12,28 @@
 stabilizer = 3.0
 gradient_energy = 2.0
 walk_step = 0.16
+
+
+def cut_along(x, dim, devices):
+    before, after = (x.shape[:dim], x.shape[dim + 1 :])
+    return jnp.moveaxis(x.reshape(*before, devices, -1, *after), dim, 0)
+
+
+def laid_out(pieces, dim):
+    pieces = jnp.moveaxis(pieces, 0, dim)
+    shape = pieces.shape
+    return pieces.reshape(*shape[:dim], shape[dim] * shape[dim + 1], *shape[dim + 2 :])
+
+
+def pairwise_exchange(x, axis, split_dim, concat_dim):
+    size, place = (lax.axis_size(axis), lax.axis_index(axis))
+    parts = cut_along(x, split_dim, size)
+    done = [parts[place]]
+    for step in range(1, size):
+        sent = parts[place ^ step]
+        done.append(lax.ppermute(sent, axis, [(i, i ^ step) for i in range(size)]))
+    parts = jnp.stack(done)[place ^ jnp.arange(size)]
+    return laid_out(parts, concat_dim)
 
 
 def with_halo(array, sides, width):
@@ -92,7 +114,7 @@
     real_part = product(form, fields, cosine_y)
     imag_part = -product(form, fields, sine_y)
     pair = (
-        lax.all_to_all(real_part, "wide", split_axis=3, concat_axis=2, tiled=True),
+        pairwise_exchange(real_part, "wide", 3, 2),
         lax.all_to_all(imag_part, "wide", split_axis=3, concat_axis=2, tiled=True),
     )
     forward_real_part, forward_imag_part = pair

time: 1480 us -> 1730 us (1.17)
  waiting for transfers between devices: 383 us -> 611 us
  local copies, waits for them, and re-layouts: 443 us -> 494 us
  other arithmetic: 196 us -> 168 us
    ppermute x0 -> x7, waiting for transfers between devices: none -> 427 us  [pairwise_exchange(): done.append(lax.ppermute(sent, axis, [(i, i ^ step) for i in range(size)]))]
    all_to_all x1 -> x0, waiting for transfers between devices: 123 us -> none  [per_device(): lax.all_to_all(real_part, 'wide', split_axis=3, concat_axis=2, tiled=True)]
    all_to_all x1, waiting for transfers between devices: 79.8 us -> 0.01 us  [per_device(): lax.all_to_all(imag_part, 'wide', split_axis=3, concat_axis=2, tiled=True)]
    another operation x0 -> x2, local copies, waits for them, and re-layouts: none -> 60.6 us
    all_to_all x3 -> x0, local copies, waits for them, and re-layouts: 32.6 us -> none  [per_device(): lax.all_to_all(real_part, 'wide', split_axis=3, concat_axis=2, tiled=True)]
    reshape x0 -> x2, local copies, waits for them, and re-layouts: none -> 27.1 us  [the longest x1 14.2 us: laid_out(): pieces.reshape(*shape[:dim], shape[dim] * shape[dim + 1], *shape[dim + 2:])]
    all_to_all x1 -> x0, other arithmetic: 26.3 us -> none  [per_device(): lax.all_to_all(real_part, 'wide', split_axis=3, concat_axis=2, tiled=True)]
    unnamed x42 -> x51, local copies, waits for them, and re-layouts: 165 us -> 146 us
  transfers between devices with their start and end apart: 24 -> 30, of which waited for: 21 -> 27; matrix products, arithmetic and copies ran while one was open for 34% -> 29% of each run, Pallas kernels for 0% -> 0%
where the time goes in v1:
time: 1730 us; the launch traced here: 1720 us
  waiting for transfers between devices  611 us (35%)
  local copies, waits for them, and re-layouts  494 us (29%)
  matrix products  324 us (19%)
  other arithmetic  168 us (10%)
  starting transfers between devices  71.5 us (4%)
  blocking collectives  46.4 us (3%)
    ppermute x7, waiting for transfers between devices, pairwise_exchange(): done.append(lax.ppermute(sent, axis, [(i, i ^ step) for i in range(size)]))  427 us
    dot_general x20, matrix products, product(): return jnp.einsum(form, left, right, precision=lax.Precision.HIGHEST)  324 us
    unnamed x51, local copies, waits for them, and re-layouts  146 us
    another operation x1, local copies, waits for them, and re-layouts  59.1 us
    psum x1, blocking collectives, per_device(): flux = lax.psum(jnp.sum(lower), ('thick', 'wide')) / (NX * NY)  46.4 us
    all_to_all x1, waiting for transfers between devices, per_device(): lax.all_to_all(pair[1], 'wide', split_axis=1, concat_axis=2, tiled=True)  46.4 us
    all_to_all x1, waiting for transfers between devices, per_device(): lax.all_to_all(pair[0], 'wide', split_axis=1, concat_axis=2, tiled=True)  42.2 us
  transfers between devices with their start and end apart: 30, of which 27 were waited for; matrix products, arithmetic and copies ran while one was open for 29% of the time, Pallas kernels for 0%

profile of v1, /device:TPU:12, one launch (start us, length us, event | category | flops | bytes accessed | tf_op | source)
XLA Modules:
  0.0 1717.8 jit_solution(15351538063232763592)
XLA Ops:
  5.6 33.4 %fusion.63 = f32[2,32,64,512]{3,2,1,0:T(8,128)} fusion(f32[1,32,64,512]{3,2,1,0:T(8,128)S(1)} %fusion.5, f32[1,32,64,512]{3,2,1,0:T(8,128)S(1)} %bitcast.227), kind=kOutput, calls=%fused_computation.115 | convolution fusion | flops 12892766208 | bytes 16777216 | tf_op jit(solution)/shard_map/fzxy,yk->fzxk/dot_general | solution.py:65
  39.0 16.3 copy.28
  55.3 15.4 reshape.138
  77.2 25.5 %fusion.1 = f32[2,32,64,512]{3,2,1,0:T(8,128)} fusion(f32[1,32,64,512]{3,2,1,0:T(8,128)} %copy-done.5, f32[1,32,64,512]{3,2,1,0:T(8,128)} %bitcast.226), kind=kOutput, calls=%fused_computation.12 | convolution fusion | flops 12890669056 | bytes 16777216 | tf_op jit(solution)/shard_map/fzxy,yk->fzxk/dot_general | solution.py:65
  102.7 12.9 reshape.120
  115.6 59.1 %constant_dynamic-slice_fusion = (f32[2,32,64,1,64]{4,3,2,1,0:T(1,128)}, f32[2,32,64,1,64]{4,3,2,1,0:T(1,128)}, f32[2,32,64,1,64]{4,3,2,1,0:T(1,128)}, f32[2,32,...) fusion(f32[2,32,64,8,64]{4,3,2,1,0:T(8,128)} %reshape.120, ...), kind=kLoop, calls=%fused_computation.216 | loop fusion | bytes 16777248 | tf_op jit(solution)/shard_map/dynamic-slice.7
  183.6 74.9 %collective-permute-done = f32[2,32,64,64]{3,2,1,0:T(8,128)S(1)} collective-permute-done((f32[2,32,64,64]{3,2,1,0:T(8,128)}, f32[2,32,64,64]{3,2,1,0:T(8,128)S(1)}, u32[]{:S(2)}, u32[]{:S(2)}) %collective-permute-start) | collective-permute-done | bytes 1048608 | tf_op jit(solution)/shard_map/ppermute | solution.py:34
  260.0 53.0 %collective-permute-done.1 = f32[2,32,64,64]{3,2,1,0:T(8,128)S(1)} collective-permute-done((f32[2,32,64,64]{3,2,1,0:T(8,128)}, f32[2,32,64,64]{3,2,1,0:T(8,128)S(1)}, u32[]{:S(2)}, u32[]{:S(2)}) %collective-permute-start.1) | collective-permute-done | bytes 1048608 | tf_op jit(solution)/shard_map/ppermute | solution.py:34
  314.5 41.4 %collective-permute-done.2 = f32[2,32,64,64]{3,2,1,0:T(8,128)S(1)} collective-permute-done((f32[2,32,64,64]{3,2,1,0:T(8,128)}, f32[2,32,64,64]{3,2,1,0:T(8,128)S(1)}, u32[]{:S(2)}, u32[]{:S(2)}) %collective-permute-start.2) | collective-permute-done | bytes 1048608 | tf_op jit(solution)/shard_map/ppermute | solution.py:34
  358.8 168.6 %collective-permute-done.4 = f32[2,32,64,64]{3,2,1,0:T(8,128)S(1)} collective-permute-done((f32[2,32,64,64]{3,2,1,0:T(8,128)}, f32[2,32,64,64]{3,2,1,0:T(8,128)S(1)}, u32[]{:S(2)}, u32[]{:S(2)}) %collective-permute-start.4) | collective-permute-done | bytes 1048608 | tf_op jit(solution)/shard_map/ppermute | solution.py:34
  529.0 45.7 %collective-permute-done.5 = f32[2,32,64,64]{3,2,1,0:T(8,128)S(1)} collective-permute-done((f32[2,32,64,64]{3,2,1,0:T(8,128)S(1)}, f32[2,32,64,64]{3,2,1,0:T(8,128)S(1)}, u32[]{:S(2)}, u32[]{:S(2)}) %collective-permute-start.5) | collective-permute-done | bytes 1048608 | tf_op jit(solution)/shard_map/ppermute | solution.py:34
  576.2 43.0 %collective-permute-done.6 = f32[2,32,64,64]{3,2,1,0:T(8,128)S(1)} collective-permute-done((f32[2,32,64,64]{3,2,1,0:T(8,128)S(1)}, f32[2,32,64,64]{3,2,1,0:T(8,128)S(1)}, u32[]{:S(2)}, u32[]{:S(2)}) %collective-permute-start.6) | collective-permute-done | bytes 1048608 | tf_op jit(solution)/shard_map/ppermute | solution.py:34
  620.7 13.8 gather_fusion
  634.5 17.5 %copy.27 = f32[2,32,8,64,64]{3,2,4,1,0:T(8,128)} copy(f32[2,32,8,64,64]{4,3,1,0,2:T(8,128)} %bitcast.215) | data formatting | bytes 16777216 | tf_op jit(solution)/shard_map/transpose | solution.py:23
  651.9 14.2 reshape.121
  666.6 26.7 %reduce = f32[8,262144]{1,0:T(8,128)} reduce(f32[8,1,262144]{2,1,0:T(1,128)} %all-to-all-done, f32[]{:T(128)} %broadcast.377), dimensions={1}, to_apply=%all_to_all.91.reduce_sub_computation | reduce | bytes 16777220 | tf_op jit(solution)/shard_map/all_to_all | solution.py:118
  693.4 15.7 reshape.139
  709.0 17.8 %copy.51 = f32[2,32,64,8,64]{2,3,4,1,0:T(8,128)} copy(f32[2,32,64,8,64]{2,1,0,4,3:T(8,128)} %bitcast.216) | data formatting | bytes 16777216 | tf_op jit(solution)/shard_map/all_to_all | solution.py:118
  726.8 14.2 all_to_all.94
  741.0 24.4 %fusion.73 = f32[2,32,64,512]{3,2,1,0:T(8,128)S(1)} fusion(f32[2,32,512,64]{2,3,1,0:T(8,128)} %all_to_all.94), kind=kOutput, calls=%fused_computation.138 | convolution fusion | flops 12888571904 | bytes 16777216 | tf_op jit(solution)/shard_map/fzxy,xk->fzyk/dot_general | solution.py:65
  765.4 26.0 %convolution_subtract_fusion = f32[2,32,64,512]{3,2,1,0:T(8,128)} fusion(f32[2,32,64,512]{3,2,1,0:T(8,128)S(1)} %fusion.73, f32[2,32,512,64]{2,3,1,0:T(8,128)} %reshape.121), kind=kOutput, calls=%fused_computation.116 | convolution fusion | flops 12890669056 | bytes 25165824 | tf_op jit(solution)/shard_map/fzxy,xk->fzyk/dot_general | solution.py:65
  791.4 16.3 copy.32
  807.6 14.3 reshape.142
  828.3 24.2 %fusion.75 = f32[2,32,64,512]{3,2,1,0:T(8,128)S(1)} fusion(f32[2,32,512,64]{2,3,1,0:T(8,128)} %reshape.121), kind=kOutput, calls=%fused_computation.140 | convolution fusion | flops 12888571904 | bytes 16777216 | tf_op jit(solution)/shard_map/fzxy,xk->fzyk/dot_general | solution.py:65
  852.5 26.0 %convolution_add_fusion = f32[2,32,64,512]{3,2,1,0:T(8,128)} fusion(f32[2,32,64,512]{3,2,1,0:T(8,128)S(1)} %fusion.75, f32[2,32,512,64]{2,3,1,0:T(8,128)} %all_to_all.94), kind=kOutput, calls=%fused_computation.117 | convolution fusion | flops 12890669056 | bytes 25165824 | tf_op jit(solution)/shard_map/fzxy,xk->fzyk/dot_general | solution.py:65
  878.6 16.3 copy.30
  894.8 14.3 reshape.140
  909.1 10.7 all-to-all-done.2
  927.4 28.3 %reduce.2 = f32[4,524288]{1,0:T(4,128)} reduce(f32[4,1,524288]{2,1,0:T(1,128)} %all-to-all-done.2, f32[]{:T(128)} %broadcast.377), dimensions={1}, to_apply=%all_to_all.99.reduce_sub_computation | reduce | bytes 16777220 | tf_op jit(solution)/shard_map/all_to_all | solution.py:126
  955.7 16.8 reshape.143
  972.5 16.0 copy.33
  988.5 12.1 fusion.106
  1000.6 18.2 %all-to-all-done.1 = f32[4,1,524288]{2,1,0:T(1,128)} async-done(((f32[4,1,524288]{2,1,0:T(1,128)}), f32[4,1,524288]{2,1,0:T(1,128)}, u32[]{:S(2)}, u32[]{:S(2)}) %all-to-all-start.1) | async-done | bytes 8388640 | tf_op jit(solution)/shard_map/all_to_all | solution.py:125
  1018.8 28.7 %reduce.1 = f32[4,524288]{1,0:T(4,128)} reduce(f32[4,1,524288]{2,1,0:T(1,128)} %all-to-all-done.1, f32[]{:T(128)} %broadcast.377), dimensions={1}, to_apply=%all_to_all.95.reduce_sub_computation | reduce | bytes 16777220 | tf_op jit(solution)/shard_map/all_to_all | solution.py:125
  1047.4 16.8 reshape.141
  1064.3 15.7 copy.31
  1080.0 11.2 fusion.108
  1091.3 12.3 subtract_bitcast_fusion
  1103.6 10.2 add_bitcast_fusion
  1145.8 8.6 subtract_bitcast_fusion.2
  1158.9 24.9 %all-to-all-done.4 = f32[64,128,128]{2,0,1:T(8,128)} async-done(((f32[64,128,128]{2,0,1:T(8,128)}), f32[64,128,128]{2,0,1:T(8,128)}, u32[]{:S(2)}, u32[]{:S(2)}) %all-to-all-start.4) | async-done | bytes 4194336 | tf_op jit(solution)/shard_map/all_to_all | solution.py:140
  1203.8 14.5 fusion.78
  1218.3 18.8 %all-to-all-done.3 = f32[64,128,128]{2,0,1:T(8,128)} async-done(((f32[64,128,128]{2,0,1:T(8,128)}), f32[64,128,128]{2,0,1:T(8,128)}, u32[]{:S(2)}, u32[]{:S(2)}) %all-to-all-start.3) | async-done | bytes 4194336 | tf_op jit(solution)/shard_map/all_to_all | solution.py:139
  1250.3 14.9 add_bitcast_fusion.1
  1265.2 9.2 copy.40
  1274.4 9.8 reshape.146
  1289.2 12.6 fusion.82
  1301.8 12.4 subtract_bitcast_fusion.1
  1314.2 9.2 copy.38
  1323.3 9.8 reshape.144
  1333.1 46.4 %all-to-all-done.6 = f32[8,1,131072]{2,1,0:T(1,128)} async-done(((f32[8,1,131072]{2,1,0:T(1,128)}), f32[8,1,131072]{2,1,0:T(1,128)}, u32[]{:S(2)}, u32[]{:S(2)}) %all-to-all-start.6) | async-done | bytes 4194336 | tf_op jit(solution)/shard_map/all_to_all | solution.py:146
  1392.7 14.0 reduce.4
  1406.6 8.8 reshape.147
  1415.4 11.5 copy.52
  1434.4 42.2 %all-to-all-done.5 = f32[8,1,131072]{2,1,0:T(1,128)} async-done(((f32[8,1,131072]{2,1,0:T(1,128)}), f32[8,1,131072]{2,1,0:T(1,128)}, u32[]{:S(2)}, u32[]{:S(2)}) %all-to-all-start.5) | async-done | bytes 4194336 | tf_op jit(solution)/shard_map/all_to_all | solution.py:145
  1476.6 14.2 reduce.3
  1490.7 8.8 reshape.145
  1499.5 11.5 copy.53
  1518.7 13.5 fusion.80
  1532.2 21.6 %multiply_add_fusion = (f32[32,64,512]{2,1,0:T(8,128)S(1)}, f32[32,64,512]{2,1,0:T(8,128)}) fusion(f32[32,64,512]{2,1,0:T(8,128)S(1)} %fusion.80, f32[32,64,512]{2,1,0:T(8,128)S(1)} %copy-done.9), kind=kOutput, calls=%fused_computation.110 | convolution fusion | flops 6453460992 | bytes 16777216 | tf_op jit(solution)/shard_map/zxk,ky->zxy/dot_general | solution.py:65
  1585.1 16.5 fusion.39
  1624.2 10.6 fusion.28
  1657.8 11.6 fusion.225
  1669.4 46.4 %psum.7 = f32[]{:T(128)} all-reduce(f32[]{:T(128)} %get-tuple-element.15), channel_id=1, replica_groups=mesh['thick'=4,'wide'=8] {'thick','wide'}, use_global_device_ids=true, to_apply=%region_1.2 | all-reduce | flops 1 | bytes 8 | tf_op jit(solution)/shard_map/psum | solution.py:171
  (133 shorter events, 224.6 us)
Async XLA Ops:
  0.6 4.9 copy-start.4
  3.5 2.0 copy-start.5
  70.7 595.5 %all-to-all-start = ((f32[8,1,262144]{2,1,0:T(1,128)}), f32[8,1,262144]{2,1,0:T(1,128)}, u32[]{:S(2)}, u32[]{:S(2)}) async-start(f32[8,1,262144]{2,1,0:T(1,128)} %reshape.138), calls=%async_computation | async-start | bytes 16777216 | tf_op jit(solution)/shard_map/all_to_all | solution.py:118
  174.7 83.8 %copy-start.11 = (f32[2,32,64,1,64]{4,3,2,1,0:T(1,128)S(1)}, f32[2,32,64,1,64]{4,3,2,1,0:T(1,128)}, u32[]{:S(2)}) copy-start(f32[2,32,64,1,64]{4,3,2,1,0:T(1,128)} %get-tuple-element.8) | copy-start | bytes 3145732
  174.7 83.8 %collective-permute-start = (f32[2,32,64,64]{3,2,1,0:T(8,128)}, f32[2,32,64,64]{3,2,1,0:T(8,128)S(1)}, u32[]{:S(2)}, u32[]{:S(2)}) collective-permute-start(f32[2,32,64,64]{3,2,1,0:T(8,128)} %bitcast.237), channel_id=1, source_target_pairs={{0,1},{1,0},{2,3},{3,2},{4,5},{5,4},{6,7},{7,6},{8,9},{9,8},{10,11... | collective-permute-start | bytes 3145736 | tf_op jit(solution)/shard_map/ppermute | solution.py:34
  176.3 136.7 %collective-permute-start.1 = (f32[2,32,64,64]{3,2,1,0:T(8,128)}, f32[2,32,64,64]{3,2,1,0:T(8,128)S(1)}, u32[]{:S(2)}, u32[]{:S(2)}) collective-permute-start(f32[2,32,64,64]{3,2,1,0:T(8,128)} %bitcast.236), channel_id=1, source_target_pairs={{0,2},{1,3},{2,0},{3,1},{4,6},{5,7},{6,4},{7,5},{8,10},{9,11},{10,... | collective-permute-start | bytes 3145736 | tf_op jit(solution)/shard_map/ppermute | solution.py:34
  176.8 179.0 %collective-permute-start.2 = (f32[2,32,64,64]{3,2,1,0:T(8,128)}, f32[2,32,64,64]{3,2,1,0:T(8,128)S(1)}, u32[]{:S(2)}, u32[]{:S(2)}) collective-permute-start(f32[2,32,64,64]{3,2,1,0:T(8,128)} %bitcast.235), channel_id=1, source_target_pairs={{0,3},{1,2},{2,1},{3,0},{4,7},{5,6},{6,5},{7,4},{8,11},{9,10},{10,... | collective-permute-start | bytes 3145736 | tf_op jit(solution)/shard_map/ppermute | solution.py:34
  178.3 179.1 %collective-permute-start.3 = (f32[2,32,64,64]{3,2,1,0:T(8,128)}, f32[2,32,64,64]{3,2,1,0:T(8,128)S(1)}, u32[]{:S(2)}, u32[]{:S(2)}) collective-permute-start(f32[2,32,64,64]{3,2,1,0:T(8,128)} %bitcast.234), channel_id=1, source_target_pairs={{0,4},{1,5},{2,6},{3,7},{4,0},{5,1},{6,2},{7,3},{8,12},{9,13},{10,... | collective-permute-start | bytes 3145736 | tf_op jit(solution)/shard_map/ppermute | solution.py:34
  180.7 346.8 %collective-permute-start.4 = (f32[2,32,64,64]{3,2,1,0:T(8,128)}, f32[2,32,64,64]{3,2,1,0:T(8,128)S(1)}, u32[]{:S(2)}, u32[]{:S(2)}) collective-permute-start(f32[2,32,64,64]{3,2,1,0:T(8,128)} %bitcast.233), channel_id=1, source_target_pairs={{0,5},{1,4},{2,7},{3,6},{4,1},{5,0},{6,3},{7,2},{8,13},{9,12},{10,... | collective-permute-start | bytes 3145736 | tf_op jit(solution)/shard_map/ppermute | solution.py:34
  182.1 130.8 %copy-start.10 = (f32[2,32,64,1,64]{4,3,2,1,0:T(1,128)S(1)}, f32[2,32,64,1,64]{4,3,2,1,0:T(1,128)}, u32[]{:S(2)}) copy-start(f32[2,32,64,1,64]{4,3,2,1,0:T(1,128)} %get-tuple-element.7) | copy-start | bytes 3145732
  258.5 316.2 %collective-permute-start.5 = (f32[2,32,64,64]{3,2,1,0:T(8,128)S(1)}, f32[2,32,64,64]{3,2,1,0:T(8,128)S(1)}, u32[]{:S(2)}, u32[]{:S(2)}) collective-permute-start(f32[2,32,64,64]{3,2,1,0:T(8,128)S(1)} %bitcast.232), channel_id=1, source_target_pairs={{0,6},{1,7},{2,4},{3,5},{4,2},{5,3},{6,0},{7,1},{8,14},{9,15},{10,... | collective-permute-start | bytes 3145736 | tf_op jit(solution)/shard_map/ppermute | solution.py:34
  313.0 306.3 %collective-permute-start.6 = (f32[2,32,64,64]{3,2,1,0:T(8,128)S(1)}, f32[2,32,64,64]{3,2,1,0:T(8,128)S(1)}, u32[]{:S(2)}, u32[]{:S(2)}) collective-permute-start(f32[2,32,64,64]{3,2,1,0:T(8,128)S(1)} %bitcast.231), channel_id=1, source_target_pairs={{0,7},{1,6},{2,5},{3,4},{4,3},{5,2},{6,1},{7,0},{8,15},{9,14},{10,... | collective-permute-start | bytes 3145736 | tf_op jit(solution)/shard_map/ppermute | solution.py:34
  822.0 97.8 %all-to-all-start.2 = ((f32[4,1,524288]{2,1,0:T(1,128)}), f32[4,1,524288]{2,1,0:T(1,128)}, u32[]{:S(2)}, u32[]{:S(2)}) async-start(f32[4,1,524288]{2,1,0:T(1,128)} %reshape.142), calls=%async_computation.2 | async-start | bytes 16777216 | tf_op jit(solution)/shard_map/all_to_all | solution.py:126
  919.8 99.0 %all-to-all-start.1 = ((f32[4,1,524288]{2,1,0:T(1,128)}), f32[4,1,524288]{2,1,0:T(1,128)}, u32[]{:S(2)}, u32[]{:S(2)}) async-start(f32[4,1,524288]{2,1,0:T(1,128)} %reshape.140), calls=%async_computation.1 | async-start | bytes 16777216 | tf_op jit(solution)/shard_map/all_to_all | solution.py:125
  1080.0 11.3 copy-start
  1080.0 23.6 %slice-start = ((s8[8388608]{0:T(1024)(128)(4,1)}), s8[4194304]{0:T(1024)(128)(4,1)S(1)}, s32[]{:S(2)}) async-start(s8[8388608]{0:T(1024)(128)(4,1)} %bitcast.205), calls=%async_computation.7 | async-start | bytes 8388608
  1091.3 12.3 slice-start.1
  1103.6 10.2 copy-start.6
  1113.8 5.8 copy-start.7
  1130.8 53.1 %all-to-all-start.4 = ((f32[64,128,128]{2,0,1:T(8,128)}), f32[64,128,128]{2,0,1:T(8,128)}, u32[]{:S(2)}, u32[]{:S(2)}) async-start(f32[64,128,128]{2,0,1:T(8,128)} %copy.36), calls=%async_computation.4 | async-start | bytes 8388608 | tf_op jit(solution)/shard_map/all_to_all | solution.py:140
  1183.8 53.3 %all-to-all-start.3 = ((f32[64,128,128]{2,0,1:T(8,128)}), f32[64,128,128]{2,0,1:T(8,128)}, u32[]{:S(2)}, u32[]{:S(2)}) async-start(f32[64,128,128]{2,0,1:T(8,128)} %copy.34), calls=%async_computation.3 | async-start | bytes 8388608 | tf_op jit(solution)/shard_map/all_to_all | solution.py:139
  1284.2 95.3 %all-to-all-start.6 = ((f32[8,1,131072]{2,1,0:T(1,128)}), f32[8,1,131072]{2,1,0:T(1,128)}, u32[]{:S(2)}, u32[]{:S(2)}) async-start(f32[8,1,131072]{2,1,0:T(1,128)} %reshape.146), calls=%async_computation.6 | async-start | bytes 8388608 | tf_op jit(solution)/shard_map/all_to_all | solution.py:146
  1289.2 12.7 copy-start.1
  1379.5 97.0 %all-to-all-start.5 = ((f32[8,1,131072]{2,1,0:T(1,128)}), f32[8,1,131072]{2,1,0:T(1,128)}, u32[]{:S(2)}, u32[]{:S(2)}) async-start(f32[8,1,131072]{2,1,0:T(1,128)} %reshape.144), calls=%async_computation.5 | async-start | bytes 8388608 | tf_op jit(solution)/shard_map/all_to_all | solution.py:145
  1387.6 4.4 collective-permute-start.7
  1387.6 168.7 %collective-permute-start.8 = (f32[1,64,512]{2,1,0:T(8,128)S(1)}, f32[1,64,512]{2,1,0:T(8,128)S(1)}, u32[]{:S(2)}, u32[]{:S(2)}) collective-permute-start(f32[1,64,512]{2,1,0:T(8,128)S(1)} %get-tuple-element.49), channel_id=1, source_target_pairs={{8,0},{16,8},{24,16},{0,24},{9,1},{17,9},{25,17},{1,25},{10,2},{18... | collective-permute-start | bytes 393224 | tf_op jit(solution)/shard_map/ppermute | solution.py:47
  1518.7 13.5 copy-start.9
  1518.7 37.0 %slice-start.2 = ((s8[4456448]{0:T(1024)(128)(4,1)}), s8[4194304]{0:T(1024)(128)(4,1)S(1)}, s32[]{:S(2)}) async-start(s8[4456448]{0:T(1024)(128)(4,1)} %bitcast.229), calls=%async_computation.9 | async-start | bytes 8388608
  1532.2 23.4 %slice-start.3 = ((s8[4456448]{0:T(1024)(128)(4,1)}), s8[262144]{0:T(1024)(128)(4,1)S(1)}, s32[]{:S(2)}) async-start(s8[4456448]{0:T(1024)(128)(4,1)} %bitcast.229), calls=%async_computation.10 | async-start | bytes 524288
  1532.2 23.4 %copy-start.8 = (f32[32,64,512]{2,1,0:T(8,128)S(1)}, f32[32,64,512]{2,1,0:T(8,128)}, u32[]{:S(2)}) copy-start(f32[32,64,512]{2,1,0:T(8,128)} %param.3) | copy-start | bytes 12582916
  1553.8 4.4 collective-permute-start.11
  1553.9 4.7 collective-permute-start.12
  1558.7 6.2 collective-permute-start.13
  1559.4 6.5 collective-permute-start.14
  1562.4 5.1 collective-permute-start.10
  1564.4 6.0 collective-permute-start.9
  1601.5 13.4 copy-start.2
  1602.7 4.4 collective-permute-start.15
  1602.7 4.5 collective-permute-start.16
  1608.5 5.9 collective-permute-start.17
  1608.6 6.4 collective-permute-start.18
  1634.8 4.4 collective-permute-start.19
  1635.0 4.7 collective-permute-start.20
  1639.8 5.9 collective-permute-start.21
  1640.5 6.5 collective-permute-start.22
  1655.6 2.2 copy-start.3
